TPU v7x, 32 devices: a whole 2x2x4 slice. The times are simulated.
32 devices in a mesh: seq: 8 (over y, x, core), tensor: 4 (over z).
Axes of the slice: x: 2, y: 2, z: 4, core: 2. Of those that a mesh axis runs over, the one named last changes fastest.
Arguments:
- tokens: bfloat16 [2048, 1024], P('seq'), may hold values from -12 to 12
- cache_keys: bfloat16 [2048, 1024], P('seq', 'tensor'), may hold values from -700 to 700
- cache_values: bfloat16 [2048, 1024], P('seq', 'tensor'), may hold values from -6 to 6
- joined_weight: float32 [1024, 3072], P(('seq', 'tensor')), may hold values from -0.1875 to 0.1875
- output_weight: float32 [1024, 1024], P(('seq', 'tensor')), may hold values from -0.1875 to 0.1875
- upward_weight: float32 [1024, 4096], P(('seq', 'tensor')), may hold values from -0.1875 to 0.1875
- downward_weight: float32 [1024, 4096], P(('seq', 'tensor')), may hold values from -0.09375 to 0.09375
- first_gain: float32 [1024], replicated, may hold values from 0.1 to 1.9
- second_gain: float32 [1024], replicated, may hold values from 0.1 to 1.9
- bias_table: float32 [32, 16], P(None, 'tensor'), may hold values from -4 to 4
- bucket_index: int32 [1023], replicated, may hold values from 0 to 31, as said below
- cached_lengths: int32 [8], replicated, may hold values from 0 to 256, as said below
- new_counts: int32 [8], replicated, may hold values from 1 to 256, as said below
- extend_flags: int32 [8], replicated, may hold values 0 or 1
Outputs:
- layer_out: bfloat16 [2048, 1024], P(('seq', 'tensor'))
Inputs may be any that keep to these rules, and one draw needn't show every extreme that they name: `cached_lengths`: some request has exactly 256 cached tokens. `new_counts`: slots of a request past its count are padding; some request fills all 256. `bucket_index`: entry 511 + o is the bucket of offset o; offsets o <= 0 take buckets below 16, offsets o > 0 the others, and on each side the bucket never falls as the distance grows.
All inputs are finite; a program needn't handle non-finite values.
Results may differ from a plain program's by a relative error of at most 0.015.
Values may be sent and summed in bfloat16 or wider, within the bound.
No kernel may reach another device: no remote copies, remote signals or barrier semaphores. Data moves between devices by JAX's collectives and lax.ppermute only.
A program may use at most 128 MiB of HBM per device.

v0:
```python
import jax
import jax.numpy as jnp
from jax import lax
from jax.sharding import PartitionSpec as P

EPSILON = 1e-06
FLOOR_SCORE = -1e30


def rms_rows(rows, gain):
    rows = rows.astype(jnp.float32)
    mean_square = jnp.mean(rows * rows, axis=-1, keepdims=True)
    return (rows * lax.rsqrt(mean_square + EPSILON) * gain).astype(jnp.bfloat16)


def row_adder(left_rows, block_rows):
    return jnp.dot(left_rows, block_rows, preferred_element_type=jnp.float32)


def column_maker(left_rows, block_rows):
    return lax.dot_general(
        left_rows, block_rows, (((1,), (1,)), ((), ())), preferred_element_type=jnp.float32
    )


def attend_block(
    carry_state, query_rows, query_pos, key_rows, value_rows, key_pos, key_ok, rel_rows
):
    row_top, row_total, weighted = carry_state
    head_count = rel_rows.shape[0]
    query_count = query_rows.shape[0]
    query_heads = query_rows.reshape(query_count, head_count, -1)
    key_heads = key_rows.reshape(key_rows.shape[0], head_count, -1)
    value_heads = value_rows.reshape(value_rows.shape[0], head_count, -1)
    span_size = (rel_rows.shape[1] + 1) // 2
    scores = jnp.einsum("qhd,khd->hqk", query_heads, key_heads, preferred_element_type=jnp.float32)
    offset = key_pos[None, :] - query_pos[:, None] + (span_size - 1)
    scores = scores + jnp.take(rel_rows, offset, axis=1)
    allowed = key_ok[None, None, :]
    new_top = jnp.maximum(row_top, jnp.max(jnp.where(allowed, scores, FLOOR_SCORE), axis=2))
    weights = jnp.where(allowed, jnp.exp(scores - new_top[:, :, None]), 0.0)
    rescale = jnp.exp(row_top - new_top)
    row_total = row_total * rescale + jnp.sum(weights, axis=2)
    update = jnp.einsum(
        "hqk,khd->qhd",
        weights.astype(jnp.bfloat16),
        value_heads,
        preferred_element_type=jnp.float32,
    )
    weighted = (
        weighted.reshape(query_count, head_count, -1) * jnp.transpose(rescale)[:, :, None] + update
    )
    return (new_top, row_total, weighted.reshape(query_count, -1))


def visit_block(
    carry_state, query_rows, query_pos, key_rows, value_rows, key_pos, key_ok, rel_rows
):
    return attend_block(
        carry_state, query_rows, query_pos, key_rows, value_rows, key_pos, key_ok, rel_rows
    )


def local_keys(
    carry_state,
    query_rows,
    query_pos,
    cache_rows,
    cache_vals,
    cache_pos,
    cache_ok,
    new_rows,
    new_vals,
    new_pos,
    new_ok,
    rel_rows,
):
    total_rows = cache_rows.shape[0]
    block_size = min(512, total_rows)
    block_count = total_rows // block_size

    def scan_step(carried, block_item):
        block_keys, block_values, block_pos, block_ok = block_item
        return (
            visit_block(
                carried,
                query_rows,
                query_pos,
                block_keys,
                block_values,
                block_pos,
                block_ok,
                rel_rows,
            ),
            None,
        )

    blocks = (
        cache_rows.reshape(block_count, block_size, -1),
        cache_vals.reshape(block_count, block_size, -1),
        cache_pos.reshape(block_count, block_size),
        cache_ok.reshape(block_count, block_size),
    )
    carry_state, unused = lax.scan(scan_step, carry_state, blocks)
    return visit_block(
        carry_state, query_rows, query_pos, new_rows, new_vals, new_pos, new_ok, rel_rows
    )


def shards(
    tokens,
    cache_keys,
    cache_values,
    joined_weight,
    output_weight,
    upward_weight,
    downward_weight,
    first_gain,
    second_gain,
    bias_table,
    bucket_index,
    cached_lengths,
    new_counts,
    extend_flags,
):
    tensor_size = lax.axis_size("tensor")
    seq_index = lax.axis_index("seq")
    tensor_index = lax.axis_index("tensor")
    new_rows = tokens.shape[0]
    cache_count = cache_keys.shape[0]
    used_len = cached_lengths[seq_index] * extend_flags[seq_index]
    new_count = new_counts[seq_index]
    attn_width = output_weight.shape[1]
    local_width = attn_width // tensor_size
    head_count = bias_table.shape[1]
    trainer_rows = joined_weight.shape[0]
    joined_send = joined_weight.reshape(trainer_rows, 3, tensor_size, local_width)
    joined_send = (
        jnp.transpose(joined_send, (0, 2, 1, 3))
        .reshape(trainer_rows, 3 * attn_width)
        .astype(jnp.bfloat16)
    )
    joined_mine, output_mine, upward_mine, downward_mine = (
        lax.all_to_all(joined_send, "tensor", split_axis=1, concat_axis=0, tiled=True),
        lax.all_to_all(
            output_weight.astype(jnp.bfloat16), "tensor", split_axis=1, concat_axis=0, tiled=True
        ),
        lax.all_to_all(
            upward_weight.astype(jnp.bfloat16), "tensor", split_axis=1, concat_axis=0, tiled=True
        ),
        lax.all_to_all(
            downward_weight.astype(jnp.bfloat16), "tensor", split_axis=1, concat_axis=0, tiled=True
        ),
    )
    normed = rms_rows(tokens, first_gain)
    projected = row_adder(normed, lax.all_gather(joined_mine, "seq", axis=0, tiled=True)).astype(
        jnp.bfloat16
    )
    query_rows = projected[:, :local_width]
    key_new = projected[:, local_width : 2 * local_width]
    value_new = projected[:, 2 * local_width :]
    bucket_hot = (
        bucket_index[:, None] == jnp.arange(bias_table.shape[0], dtype=jnp.int32)[None, :]
    ).astype(jnp.float32)
    rel_rows = jnp.einsum("bh,lb->hl", bias_table, bucket_hot, precision=lax.Precision.HIGHEST)
    cache_pos = jnp.arange(cache_count, dtype=jnp.int32)
    cache_ok = cache_pos < used_len
    new_slots = jnp.arange(new_rows, dtype=jnp.int32)
    new_pos = used_len + new_slots
    new_ok = new_slots < new_count
    empty_state = (
        jnp.full((head_count, new_rows), FLOOR_SCORE, jnp.float32),
        jnp.zeros((head_count, new_rows), jnp.float32),
        jnp.zeros((new_rows, local_width), jnp.float32),
    )
    final_top, final_total, final_sum = local_keys(
        empty_state,
        query_rows,
        new_pos,
        cache_keys,
        cache_values,
        cache_pos,
        cache_ok,
        key_new,
        value_new,
        new_pos,
        new_ok,
        rel_rows,
    )
    attention = final_sum.reshape(new_rows, head_count, -1) / jnp.transpose(final_total)[:, :, None]
    attention = attention.reshape(new_rows, local_width).astype(jnp.bfloat16)
    attended = column_maker(attention, lax.all_gather(output_mine, "seq", axis=0, tiled=True))
    share_rows = new_rows // tensor_size
    row_start = tensor_index * share_rows
    summed = lax.psum(attended.astype(jnp.bfloat16), "tensor").astype(jnp.float32)
    hidden = tokens.astype(jnp.float32) + summed
    normed_mid = rms_rows(hidden, second_gain)
    hidden_mine = lax.dynamic_slice_in_dim(hidden, row_start, share_rows, 0)
    inner = row_adder(normed_mid, lax.all_gather(upward_mine, "seq", axis=0, tiled=True))
    active = jax.nn.relu(inner).astype(jnp.bfloat16)
    feed_out = column_maker(active, lax.all_gather(downward_mine, "seq", axis=0, tiled=True))
    feed_mine = lax.psum_scatter(
        feed_out.astype(jnp.bfloat16), "tensor", scatter_dimension=0, tiled=True
    ).astype(jnp.float32)
    return (hidden_mine + feed_mine).astype(jnp.bfloat16)


def solution(mesh):
    return jax.shard_map(
        shards,
        mesh=mesh,
        in_specs=(
            P("seq", None),
            P("seq", "tensor"),
            P("seq", "tensor"),
            P(("seq", "tensor"), None),
            P(("seq", "tensor"), None),
            P(("seq", "tensor"), None),
            P(("seq", "tensor"), None),
            P(),
            P(),
            P(None, "tensor"),
            P(),
            P(),
            P(),
            P(),
        ),
        out_specs=P(("seq", "tensor"), None),
        check_vma=False,
    )
```

profile of v0, /device:TPU:0, one launch (start us, length us, event | category | flops | bytes accessed | tf_op | source)
XLA Modules:
  0.0 660.5 jit_solution(6525563530860254248)
XLA Ops:
  6.5 1.1 convert_element_type.69
  7.6 0.1 convert_element_type.70
  7.9 0.9 convert_element_type.72
  8.8 6.3 all-to-all-start
  15.1 0.6 dynamic_slice.23
  15.7 0.6 dynamic_slice.24
  17.6 0.2 fusion.29
  17.8 0.1 copy.88
  18.0 0.6 copy.97
  18.6 4.0 all-to-all-done
  22.6 3.3 all-to-all-start.1
  26.0 0.7 all-gather.4.cloned.1.call-update
  26.7 0.4 convolution_bitcast_fusion.2
  27.1 0.2 copy.64
  27.4 217.1 %gather_fusion = f32[65536,4]{1,0:T(8,128)} fusion(f32[4,1023]{0,1:T(8,128)S(1)} %copy.64, s32[65536]{0:T(1024)S(1)} %broadcast_clamp_fusion.1), kind=kCustom, calls=%fused_computation.clone | custom fusion | bytes 2359296 | tf_op jit(solution)/shard_map/while/body/eval_jaxpr/jit(_take)/gather | solution.py:38
  244.5 19.0 %copy.66 = f32[256,256,4]{0,1,2:T(8,128)S(1)} copy(f32[256,256,4]{2,1,0:T(8,128)} %bitcast.99) | data formatting | bytes 2097152 | tf_op jit(solution)/shard_map/while/body/eval_jaxpr/jit(_take)/gather | solution.py:38
  263.5 0.3 fusion.36
  263.8 0.8 copy.63
  264.5 0.8 copy.62
  265.3 0.1 copy.89
  265.5 217.1 %gather_fusion.1 = f32[65536,4]{1,0:T(8,128)} fusion(f32[4,1023]{0,1:T(8,128)S(1)} %copy.64, s32[65536]{0:T(1024)S(1)} %broadcast_clamp_fusion), kind=kCustom, calls=%fused_computation.1.clone | custom fusion | bytes 2359296 | tf_op jit(solution)/shard_map/jit(_take)/gather | solution.py:38
  482.6 19.1 %copy.73 = f32[256,256,4]{0,1,2:T(8,128)S(1)} copy(f32[256,256,4]{2,1,0:T(8,128)} %bitcast.98) | data formatting | bytes 2097152 | tf_op jit(solution)/shard_map/jit(_take)/gather | solution.py:38
  501.7 0.8 copy.70
  502.5 0.6 dynamic_slice.25
  503.1 0.8 copy.67
  503.8 0.2 fusion.6
  504.0 0.6 iota_compare_fusion.2
  504.7 9.9 %all_gather.13 = bf16[1024,256]{1,0:T(8,128)(2,1)S(1)} all-gather(bf16[128,256]{1,0:T(8,128)(2,1)S(1)} %bitcast.115), channel_id=1, replica_groups=mesh['seq'=8,'tensor'=4] {'seq'}, dimensions={0}, use_global_device_ids=true | all-gather | bytes 589824 | tf_op jit(solution)/shard_map/all_gather | solution.py:192
  514.5 2.0 convolution_convert_fusion.2
  516.6 0.7 fusion.47
  517.2 1.0 copy.61
  518.3 0.8 copy.69
  519.0 0.7 copy.74
  519.8 1.4 select_reduce_fusion.1
  521.2 0.4 select_reduce_fusion
  521.6 0.4 fusion.9
  522.1 0.3 fusion.4
  522.5 0.3 fusion.5
  522.9 1.2 convolution_convert_fusion
  524.2 20.1 %all_to_all.73 = bf16[32,4,1024]{2,0,1:T(8,128)(2,1)} all-to-all(bf16[32,4,1024]{2,0,1:T(8,128)(2,1)S(1)} %bitcast.109), channel_id=1, replica_groups=mesh['seq'=8,'tensor'=4] {'tensor'}, dimensions={1} | all-to-all | bytes 524288 | tf_op jit(solution)/shard_map/all_to_all | solution.py:148
  544.4 11.8 %all_to_all.74 = bf16[32,4,1024]{2,0,1:T(8,128)(2,1)} all-to-all(bf16[32,4,1024]{2,0,1:T(8,128)(2,1)S(1)} %bitcast.110), channel_id=1, replica_groups=mesh['seq'=8,'tensor'=4] {'tensor'}, dimensions={1} | all-to-all | bytes 524288 | tf_op jit(solution)/shard_map/all_to_all | solution.py:151
  556.2 10.4 %all-reduce.2.cloned.1.call-done = bf16[256,1024]{1,0:T(8,128)(2,1)} async-done(((bf16[256,1024]{1,0:T(8,128)(2,1)}), bf16[256,1024]{1,0:T(8,128)(2,1)}) %all-reduce.2.cloned.1.call-update) | async-done | bytes 524304 | tf_op jit(solution)/shard_map/psum | solution.py:195
  566.6 1.4 convert_add_fusion
  568.0 28.4 %all-gather.6.cloned.1.call-done = bf16[1024,1024]{1,0:T(8,128)(2,1)} async-done(((bf16[128,1024]{1,0:T(8,128)(2,1)}), bf16[1024,1024]{1,0:T(8,128)(2,1)}) %all-gather.6.cloned.1.call-update) | async-done | bytes 2097168 | tf_op jit(solution)/shard_map/all_gather | solution.py:199
  596.5 29.7 %all-gather.8.cloned.1.call-done = bf16[1024,1024]{1,0:T(8,128)(2,1)} async-done(((bf16[128,1024]{1,0:T(8,128)(2,1)}), bf16[1024,1024]{1,0:T(8,128)(2,1)}) %all-gather.8.cloned.1.call-update) | async-done | bytes 2097168 | tf_op jit(solution)/shard_map/all_gather | solution.py:201
  626.1 4.4 convolution_convert_fusion.1
  630.6 21.8 %reduce-scatter.2.cloned.1.call-done = bf16[64,1024]{1,0:T(8,128)(2,1)} async-done(((bf16[256,1024]{1,0:T(8,128)(2,1)}), bf16[64,1024]{1,0:T(8,128)(2,1)}) %reduce-scatter.2.cloned.1.call-update) | async-done | bytes 131088 | tf_op jit(solution)/shard_map/reduce_scatter | solution.py:202
  652.4 1.6 add_convert_fusion
  (65 shorter events, 0.8 us)
Async XLA Ops:
  6.5 20.1 %copy-start = (f32[32,4]{0,1:T(4,128)S(1)}, f32[32,4]{0,1:T(4,128)}, u32[]{:S(2)}) copy-start(f32[32,4]{0,1:T(4,128)} %param.25) | copy-start | bytes 1540
  6.5 8.6 %copy-start.17 = (s32[8]{0:T(128)S(1)}, s32[8]{0:T(128)}, u32[]{:S(2)}) copy-start(s32[8]{0:T(128)} %param.27) | copy-start | bytes 100
  6.5 9.1 %copy-start.18 = (s32[8]{0:T(128)S(1)}, s32[8]{0:T(128)}, u32[]{:S(2)}) copy-start(s32[8]{0:T(128)} %param.29) | copy-start | bytes 100
  6.5 11.4 %copy-start.10 = (f32[32,1024]{1,0:T(8,128)S(1)}, f32[32,1024]{1,0:T(8,128)}, u32[]{:S(2)}) copy-start(f32[32,1024]{1,0:T(8,128)} %param.20) | copy-start | bytes 393220
  7.6 19.1 %copy-start.14 = (s32[1023]{0:T(1024)S(1)}, s32[1023]{0:T(1024)}, u32[]{:S(2)}) copy-start(s32[1023]{0:T(1024)} %param.26) | copy-start | bytes 12280
  8.8 13.8 %all-to-all-start = ((bf16[32,4,768]{2,0,1:T(8,128)(2,1)}), bf16[32,4,768]{2,0,1:T(8,128)(2,1)S(1)}, u32[]{:S(2)}, u32[]{:S(2)}) async-start(bf16[32,4,768]{2,0,1:T(8,128)(2,1)} %convert_element_type.72), calls=%async_computation | async-start | bytes 393216 | tf_op jit(solution)/shard_map/all_to_all | solution.py:144
  22.6 3.3 copy-start.3
  22.6 482.1 %all-to-all-start.1 = ((bf16[32,4,256]{2,0,1:T(8,128)(2,1)}), bf16[32,4,256]{2,0,1:T(8,128)(2,1)S(1)}, u32[]{:S(2)}, u32[]{:S(2)}) async-start(bf16[32,4,256]{2,0,1:T(8,128)(2,1)} %bitcast.97), calls=%async_computation.1 | async-start | bytes 131072 | tf_op jit(solution)/shard_map/all_to_all | solution.py:145
  25.9 488.6 %all-gather.4.cloned.1.call-start = ((), (), s32[]{:S(2)}) async-start(), calls=%async_computation.5 | async-start | bytes 1769472 | tf_op jit(solution)/shard_map/all_gather | solution.py:156
  26.6 540.0 %all-reduce.2.cloned.1.call-start = ((), (), s32[]{:S(2)}) async-start(), calls=%async_computation.6 | async-start | bytes 1048576 | tf_op jit(solution)/shard_map/psum | solution.py:195
  244.5 20.1 %copy-start.11 = (bf16[256,256]{1,0:T(8,128)(2,1)S(1)}, bf16[256,256]{1,0:T(8,128)(2,1)}, u32[]{:S(2)}) copy-start(bf16[256,256]{1,0:T(8,128)(2,1)} %param.17) | copy-start | bytes 393220
  482.6 19.9 %copy-start.19 = (s32[8]{0:T(128)S(1)}, s32[8]{0:T(128)}, u32[]{:S(2)}) copy-start(s32[8]{0:T(128)} %param.28) | copy-start | bytes 100
  482.6 20.5 %copy-start.12 = (bf16[256,256]{1,0:T(8,128)(2,1)S(1)}, bf16[256,256]{1,0:T(8,128)(2,1)}, u32[]{:S(2)}) copy-start(bf16[256,256]{1,0:T(8,128)(2,1)} %param.18) | copy-start | bytes 393220
  482.6 21.2 %copy-start.2 = (bf16[256,1024]{1,0:T(8,128)(2,1)S(1)}, bf16[256,1024]{1,0:T(8,128)(2,1)}, u32[]{:S(2)}) copy-start(bf16[256,1024]{1,0:T(8,128)(2,1)} %param.16) | copy-start | bytes 1572868
  482.6 31.9 %copy-start.15 = (f32[1024]{0:T(1024)S(1)}, f32[1024]{0:T(1024)}, u32[]{:S(2)}) copy-start(f32[1024]{0:T(1024)} %param.23) | copy-start | bytes 12292
  519.0 2.1 copy-start.8
  519.8 1.4 copy-start.9
  521.2 0.9 copy-start.7
  521.6 0.9 copy-start.13
  522.4 1.7 copy-start.4
  522.8 21.5 %copy-start.5 = (f32[32,4096]{1,0:T(8,128)S(1)}, f32[32,4096]{1,0:T(8,128)}, u32[]{:S(2)}) copy-start(f32[32,4096]{1,0:T(8,128)} %param.22) | copy-start | bytes 1572868
  524.0 72.4 %all-gather.6.cloned.1.call-start = ((), (), s32[]{:S(2)}) async-start(), calls=%async_computation.7 | async-start | bytes 2359296 | tf_op jit(solution)/shard_map/all_gather | solution.py:199
  544.3 81.8 %copy-start.16 = (f32[1024]{0:T(1024)S(1)}, f32[1024]{0:T(1024)}, u32[]{:S(2)}) copy-start(f32[1024]{0:T(1024)} %param.24) | copy-start | bytes 12292
  544.3 81.8 %all-gather.8.cloned.1.call-start = ((), (), s32[]{:S(2)}) async-start(), calls=%async_computation.8 | async-start | bytes 2359296 | tf_op jit(solution)/shard_map/all_gather | solution.py:201
  556.2 96.2 %reduce-scatter.2.cloned.1.call-start = ((), (), s32[]{:S(2)}) async-start(), calls=%async_computation.9 | async-start | bytes 655360 | tf_op jit(solution)/shard_map/reduce_scatter | solution.py:202
  566.6 59.5 %copy-start.6 = (bf16[256,1024]{1,0:T(8,128)(2,1)S(1)}, bf16[256,1024]{1,0:T(8,128)(2,1)}, u32[]{:S(2)}) copy-start(bf16[256,1024]{1,0:T(8,128)(2,1)} %all-reduce.2.cloned.1.call-done) | copy-start | bytes 1572868
  626.1 27.8 %copy-start.1 = (f32[32,4]{0,1:T(4,128)S(1)}, f32[32,4]{0,1:T(4,128)}, u32[]{:S(2)}) copy-start(f32[32,4]{0,1:T(4,128)} %param.25) | copy-start | bytes 1540
Sparse Core Ops, SparseCore 0:
  28.6 27.1 all-gather.3
  524.2 42.4 all-reduce.1
  568.5 27.8 all-gather.5
  598.2 27.8 all-gather.7
  630.7 21.6 reduce-scatter.1
where the time goes:
time: 661 us; the launch traced here: 660 us
  local copies, waits for them, and re-layouts  483 us (73%)
  waiting for transfers between devices  95 us (14%)
  blocking collectives  41.7 us (6%)
  between operations  14.8 us (2%)
  matrix products  10.4 us (2%)
  starting transfers between devices  9.81 us (1%)
    gather x4, local copies, waits for them, and re-layouts, attend_block(): scores = scores + jnp.take(rel_rows, offset, axis=1)  472 us
    all_gather x1, waiting for transfers between devices, shards(): lax.all_gather(downward_mine, 'seq', axis=0, tiled=True)  29.7 us
    all_gather x1, waiting for transfers between devices, shards(): lax.all_gather(upward_mine, 'seq', axis=0, tiled=True)  28.4 us
    reduce_scatter x1, waiting for transfers between devices, shards(): lax.psum_scatter(feed_out.astype(jnp.bfloat16), 'tensor', scatter_dimensi...  21.8 us
    all_to_all x1, blocking collectives, shards(): lax.all_to_all(upward_weight.astype(jnp.bfloat16), 'tensor', split_axis=1...  20.1 us
  transfers between devices with their start and end apart: 7, of which 5 were waited for; matrix products, arithmetic and copies ran while one was open for 73% of the time, Pallas kernels for 0%

commit v1 on v0

--- a/solution.py
+++ b/solution.py
@@ -1,3 +1,4 @@
+import functools
 import jax
 import jax.numpy as jnp
 from jax import lax
@@ -5,6 +6,23 @@
 
 EPSILON = 1e-06
 FLOOR_SCORE = -1e30
+
+
+def advance_leaves(content, named_axis):
+    outer = lax.axis_index(named_axis)
+    tile_out = lax.axis_size(named_axis)
+    built, finding = (tile_out, outer)
+    even, after = (content, 1)
+    while after < built:
+        found_now = lax.ppermute(even, named_axis, [(i, i ^ after) for i in range(built)])
+        v_now = jnp.concatenate([even, found_now], axis=0)
+        main = jnp.concatenate([found_now, even], axis=0)
+        even = jnp.where(finding & after == 0, v_now, main)
+        after = 2 * after
+    return even
+
+
+task_compute = functools.partial(advance_leaves, named_axis="seq")
 
 
 def rms_rows(rows, gain):
@@ -198,7 +216,7 @@
     hidden_mine = lax.dynamic_slice_in_dim(hidden, row_start, share_rows, 0)
     inner = row_adder(normed_mid, lax.all_gather(upward_mine, "seq", axis=0, tiled=True))
     active = jax.nn.relu(inner).astype(jnp.bfloat16)
-    feed_out = column_maker(active, lax.all_gather(downward_mine, "seq", axis=0, tiled=True))
+    feed_out = column_maker(active, task_compute(downward_mine))
     feed_mine = lax.psum_scatter(
         feed_out.astype(jnp.bfloat16), "tensor", scatter_dimension=0, tiled=True
     ).astype(jnp.float32)

time: 661 us -> 639 us (0.967)
  waiting for transfers between devices: 95 us -> 70.3 us
    ppermute x0 -> x3, waiting for transfers between devices: none -> 44.6 us  [advance_leaves(): lax.ppermute(even, named_axis, [(i, i ^ after) for i in range(built)])]
    all_gather x1 -> x0, waiting for transfers between devices: 29.7 us -> none  [shards(): lax.all_gather(downward_mine, 'seq', axis=0, tiled=True)]
    all_gather x1, waiting for transfers between devices: 28.4 us -> 0.05 us  [shards(): lax.all_gather(upward_mine, 'seq', axis=0, tiled=True)]
    psum x1, waiting for transfers between devices: 10.4 us -> 0.01 us  [shards(): lax.psum(attended.astype(jnp.bfloat16), 'tensor').astype(jnp.float32)]
  transfers between devices with their start and end apart: 7 -> 9, of which waited for: 5 -> 6; matrix products, arithmetic and copies ran while one was open for 73% -> 76% of each run, Pallas kernels for 0% -> 0%
where the time goes in v1:
time: 639 us; the launch traced here: 638 us
  local copies, waits for them, and re-layouts  483 us (76%)
  waiting for transfers between devices  70.3 us (11%)
  blocking collectives  41.2 us (6%)
  between operations  14.8 us (2%)
  starting transfers between devices  12.3 us (2%)
  matrix products  10.4 us (2%)
  other arithmetic  6.46 us (1%)
    gather x4, local copies, waits for them, and re-layouts, attend_block(): scores = scores + jnp.take(rel_rows, offset, axis=1)  472 us
    ppermute x3, waiting for transfers between devices, advance_leaves(): lax.ppermute(even, named_axis, [(i, i ^ after) for i in range(built)])  44.6 us
    reduce_scatter x1, waiting for transfers between devices, shards(): lax.psum_scatter(feed_out.astype(jnp.bfloat16), 'tensor', scatter_dimensi...  20.9 us
    all_to_all x1, blocking collectives, shards(): lax.all_to_all(upward_weight.astype(jnp.bfloat16), 'tensor', split_axis=1...  20.1 us
  transfers between devices with their start and end apart: 9, of which 6 were waited for; matrix products, arithmetic and copies ran while one was open for 76% of the time, Pallas kernels for 0%

profile of v1, /device:TPU:0, one launch (start us, length us, event | category | flops | bytes accessed | tf_op | source)
XLA Modules:
  0.0 638.2 jit_solution(548631739487405836)
XLA Ops:
  6.5 1.1 convert_element_type.69
  7.9 0.9 convert_element_type.72
  8.8 6.3 all-to-all-start
  15.1 0.6 dynamic_slice.23
  15.7 0.6 dynamic_slice.24
  17.6 0.2 fusion.37
  18.0 0.6 copy.97
  18.6 4.0 all-to-all-done
  22.6 3.3 all-to-all-start.1
  26.0 0.7 all-gather.3.cloned.1.call-update
  26.7 0.4 convolution_bitcast_fusion.2
  27.1 0.2 copy.64
  27.4 217.1 %gather_fusion = f32[65536,4]{1,0:T(8,128)} fusion(f32[4,1023]{0,1:T(8,128)S(1)} %copy.64, s32[65536]{0:T(1024)S(1)} %broadcast_clamp_fusion.1), kind=kCustom, calls=%fused_computation.clone | custom fusion | bytes 2359296 | tf_op jit(solution)/shard_map/while/body/eval_jaxpr/jit(_take)/gather | solution.py:56
  244.5 19.0 %copy.66 = f32[256,256,4]{0,1,2:T(8,128)S(1)} copy(f32[256,256,4]{2,1,0:T(8,128)} %bitcast.98) | data formatting | bytes 2097152 | tf_op jit(solution)/shard_map/while/body/eval_jaxpr/jit(_take)/gather | solution.py:56
  263.5 0.3 fusion.44
  263.8 0.8 copy.63
  264.5 0.8 copy.62
  265.5 217.1 %gather_fusion.1 = f32[65536,4]{1,0:T(8,128)} fusion(f32[4,1023]{0,1:T(8,128)S(1)} %copy.64, s32[65536]{0:T(1024)S(1)} %broadcast_clamp_fusion), kind=kCustom, calls=%fused_computation.1.clone | custom fusion | bytes 2359296 | tf_op jit(solution)/shard_map/jit(_take)/gather | solution.py:56
  482.6 19.1 %copy.73 = f32[256,256,4]{0,1,2:T(8,128)S(1)} copy(f32[256,256,4]{2,1,0:T(8,128)} %bitcast.97) | data formatting | bytes 2097152 | tf_op jit(solution)/shard_map/jit(_take)/gather | solution.py:56
  501.7 0.8 copy.70
  502.5 0.6 dynamic_slice.25
  503.1 0.8 copy.67
  503.8 0.2 fusion.14
  504.0 0.6 iota_compare_fusion.2
  504.7 9.9 %all_gather.10 = bf16[1024,256]{1,0:T(8,128)(2,1)S(1)} all-gather(bf16[128,256]{1,0:T(8,128)(2,1)S(1)} %bitcast.115), channel_id=1, replica_groups=mesh['seq'=8,'tensor'=4] {'seq'}, dimensions={0}, use_global_device_ids=true | all-gather | bytes 589824 | tf_op jit(solution)/shard_map/all_gather | solution.py:210
  514.5 2.0 convolution_convert_fusion.1
  516.6 0.7 fusion.56
  517.2 1.0 copy.61
  518.3 0.8 copy.69
  519.0 0.7 copy.74
  519.8 1.4 select_reduce_fusion.1
  521.2 0.4 select_reduce_fusion
  521.6 0.4 fusion.17
  522.1 0.3 fusion.12
  522.5 0.3 fusion.13
  522.9 1.1 convolution_convert_fusion
  524.1 20.1 %all_to_all.73 = bf16[32,4,1024]{2,0,1:T(8,128)(2,1)} all-to-all(bf16[32,4,1024]{2,0,1:T(8,128)(2,1)S(1)} %bitcast.107), channel_id=1, replica_groups=mesh['seq'=8,'tensor'=4] {'tensor'}, dimensions={1} | all-to-all | bytes 524288 | tf_op jit(solution)/shard_map/all_to_all | solution.py:166
  544.4 11.3 %all_to_all.74 = bf16[32,4,1024]{2,0,1:T(8,128)(2,1)S(1)} all-to-all(bf16[32,4,1024]{2,0,1:T(8,128)(2,1)S(1)} %bitcast.108), channel_id=1, replica_groups=mesh['seq'=8,'tensor'=4] {'tensor'}, dimensions={1} | all-to-all | bytes 524288 | tf_op jit(solution)/shard_map/all_to_all | solution.py:169
  555.6 1.5 collective-permute-done
  557.3 1.4 collective-permute-start.1
  558.7 12.7 %collective-permute-done.1 = bf16[256,1024]{1,0:T(8,128)(2,1)S(1)} collective-permute-done((bf16[256,1024]{1,0:T(8,128)(2,1)S(1)}, bf16[256,1024]{1,0:T(8,128)(2,1)S(1)}, u32[]{:S(2)}, u32[]{:S(2)}) %collective-permute-start.1) | collective-permute-done | bytes 524320 | tf_op jit(solution)/shard_map/ppermute | solution.py:17
  571.3 0.5 maximum_select_fusion.4
  571.8 1.2 collective-permute-start.2
  573.0 1.4 convert_add_fusion
  574.4 30.4 %collective-permute-done.2 = bf16[512,1024]{1,0:T(8,128)(2,1)} collective-permute-done((bf16[512,1024]{1,0:T(8,128)(2,1)S(1)}, bf16[512,1024]{1,0:T(8,128)(2,1)}, u32[]{:S(2)}, u32[]{:S(2)}) %collective-permute-start.2) | collective-permute-done | bytes 1048608 | tf_op jit(solution)/shard_map/ppermute | solution.py:17
  604.9 4.3 fusion.7
  609.2 20.9 %reduce-scatter.2.cloned.1.call-done = bf16[64,1024]{1,0:T(8,128)(2,1)} async-done(((bf16[256,1024]{1,0:T(8,128)(2,1)}), bf16[64,1024]{1,0:T(8,128)(2,1)}) %reduce-scatter.2.cloned.1.call-update) | async-done | bytes 131088 | tf_op jit(solution)/shard_map/reduce_scatter | solution.py:220
  630.1 1.6 add_convert_fusion
  (70 shorter events, 1.3 us)
Async XLA Ops:
  6.5 20.1 %copy-start = (f32[32,4]{0,1:T(4,128)S(1)}, f32[32,4]{0,1:T(4,128)}, u32[]{:S(2)}) copy-start(f32[32,4]{0,1:T(4,128)} %param.25) | copy-start | bytes 1540
  6.5 8.6 %copy-start.17 = (s32[8]{0:T(128)S(1)}, s32[8]{0:T(128)}, u32[]{:S(2)}) copy-start(s32[8]{0:T(128)} %param.27) | copy-start | bytes 100
  6.5 9.1 %copy-start.18 = (s32[8]{0:T(128)S(1)}, s32[8]{0:T(128)}, u32[]{:S(2)}) copy-start(s32[8]{0:T(128)} %param.29) | copy-start | bytes 100
  6.5 11.4 %copy-start.10 = (f32[32,1024]{1,0:T(8,128)S(1)}, f32[32,1024]{1,0:T(8,128)}, u32[]{:S(2)}) copy-start(f32[32,1024]{1,0:T(8,128)} %param.20) | copy-start | bytes 393220
  7.6 19.1 %copy-start.14 = (s32[1023]{0:T(1024)S(1)}, s32[1023]{0:T(1024)}, u32[]{:S(2)}) copy-start(s32[1023]{0:T(1024)} %param.26) | copy-start | bytes 12280
  8.8 13.8 %all-to-all-start = ((bf16[32,4,768]{2,0,1:T(8,128)(2,1)}), bf16[32,4,768]{2,0,1:T(8,128)(2,1)S(1)}, u32[]{:S(2)}, u32[]{:S(2)}) async-start(bf16[32,4,768]{2,0,1:T(8,128)(2,1)} %convert_element_type.72), calls=%async_computation | async-start | bytes 393216 | tf_op jit(solution)/shard_map/all_to_all | solution.py:162
  22.6 3.3 copy-start.3
  22.6 482.1 %all-to-all-start.1 = ((bf16[32,4,256]{2,0,1:T(8,128)(2,1)}), bf16[32,4,256]{2,0,1:T(8,128)(2,1)S(1)}, u32[]{:S(2)}, u32[]{:S(2)}) async-start(bf16[32,4,256]{2,0,1:T(8,128)(2,1)} %bitcast.96), calls=%async_computation.1 | async-start | bytes 131072 | tf_op jit(solution)/shard_map/all_to_all | solution.py:163
  25.9 488.6 %all-gather.3.cloned.1.call-start = ((), (), s32[]{:S(2)}) async-start(), calls=%async_computation.5 | async-start | bytes 1769472 | tf_op jit(solution)/shard_map/all_gather | solution.py:174
  26.6 546.4 %all-reduce.2.cloned.1.call-start = ((), (), s32[]{:S(2)}) async-start(), calls=%async_computation.6 | async-start | bytes 1048576 | tf_op jit(solution)/shard_map/psum | solution.py:213
  244.5 20.1 %copy-start.11 = (bf16[256,256]{1,0:T(8,128)(2,1)S(1)}, bf16[256,256]{1,0:T(8,128)(2,1)}, u32[]{:S(2)}) copy-start(bf16[256,256]{1,0:T(8,128)(2,1)} %param.17) | copy-start | bytes 393220
  482.6 19.9 %copy-start.19 = (s32[8]{0:T(128)S(1)}, s32[8]{0:T(128)}, u32[]{:S(2)}) copy-start(s32[8]{0:T(128)} %param.28) | copy-start | bytes 100
  482.6 20.5 %copy-start.12 = (bf16[256,256]{1,0:T(8,128)(2,1)S(1)}, bf16[256,256]{1,0:T(8,128)(2,1)}, u32[]{:S(2)}) copy-start(bf16[256,256]{1,0:T(8,128)(2,1)} %param.18) | copy-start | bytes 393220
  482.6 21.2 %copy-start.2 = (bf16[256,1024]{1,0:T(8,128)(2,1)S(1)}, bf16[256,1024]{1,0:T(8,128)(2,1)}, u32[]{:S(2)}) copy-start(bf16[256,1024]{1,0:T(8,128)(2,1)} %param.16) | copy-start | bytes 1572868
  482.6 31.9 %copy-start.15 = (f32[1024]{0:T(1024)S(1)}, f32[1024]{0:T(1024)}, u32[]{:S(2)}) copy-start(f32[1024]{0:T(1024)} %param.23) | copy-start | bytes 12292
  519.0 2.1 copy-start.8
  519.8 1.4 copy-start.9
  521.2 0.9 copy-start.7
  521.6 0.9 copy-start.13
  522.4 1.7 copy-start.4
  522.8 21.5 %copy-start.5 = (f32[32,4096]{1,0:T(8,128)S(1)}, f32[32,4096]{1,0:T(8,128)}, u32[]{:S(2)}) copy-start(f32[32,4096]{1,0:T(8,128)} %param.22) | copy-start | bytes 1572868
  524.0 80.8 %all-gather.5.cloned.1.call-start = ((), (), s32[]{:S(2)}) async-start(), calls=%async_computation.7 | async-start | bytes 2359296 | tf_op jit(solution)/shard_map/all_gather | solution.py:217
  544.3 85.8 %reduce-scatter.2.cloned.1.call-start = ((), (), s32[]{:S(2)}) async-start(), calls=%async_computation.8 | async-start | bytes 655360 | tf_op jit(solution)/shard_map/reduce_scatter | solution.py:220
  555.6 1.5 collective-permute-start
  557.3 14.0 %collective-permute-start.1 = (bf16[256,1024]{1,0:T(8,128)(2,1)S(1)}, bf16[256,1024]{1,0:T(8,128)(2,1)S(1)}, u32[]{:S(2)}, u32[]{:S(2)}) collective-permute-start(bf16[256,1024]{1,0:T(8,128)(2,1)S(1)} %maximum_select_fusion.5), channel_id=1, source_target_pairs={{0,8},{4,12},{8,0},{12,4},{16,24},{20,28},{24,16},{28,20},{1,9},{5... | collective-permute-start | bytes 1572872 | tf_op jit(solution)/shard_map/ppermute | solution.py:17
  558.7 46.2 %copy-start.16 = (f32[1024]{0:T(1024)S(1)}, f32[1024]{0:T(1024)}, u32[]{:S(2)}) copy-start(f32[1024]{0:T(1024)} %param.24) | copy-start | bytes 12292
  571.8 33.0 %collective-permute-start.2 = (bf16[512,1024]{1,0:T(8,128)(2,1)S(1)}, bf16[512,1024]{1,0:T(8,128)(2,1)}, u32[]{:S(2)}, u32[]{:S(2)}) collective-permute-start(bf16[512,1024]{1,0:T(8,128)(2,1)S(1)} %maximum_select_fusion.4), channel_id=1, source_target_pairs={{0,16},{4,20},{8,24},{12,28},{16,0},{20,4},{24,8},{28,12},{1,17},{... | collective-permute-start | bytes 3145736 | tf_op jit(solution)/shard_map/ppermute | solution.py:17
  573.0 31.9 %copy-start.6 = (bf16[256,1024]{1,0:T(8,128)(2,1)S(1)}, bf16[256,1024]{1,0:T(8,128)(2,1)}, u32[]{:S(2)}) copy-start(bf16[256,1024]{1,0:T(8,128)(2,1)} %all-reduce.2.cloned.1.call-done) | copy-start | bytes 1572868
  604.8 26.8 %copy-start.1 = (f32[32,4]{0,1:T(4,128)S(1)}, f32[32,4]{0,1:T(4,128)}, u32[]{:S(2)}) copy-start(f32[32,4]{0,1:T(4,128)} %param.25) | copy-start | bytes 1540
Sparse Core Ops, SparseCore 0:
  28.6 27.1 all-gather.2
  524.1 42.4 all-reduce.1
  568.5 36.2 all-gather.4
  609.3 20.7 reduce-scatter.1
